TPU v7x, 256 devices: a whole 4x4x8 slice. The times are simulated.
256 devices in a mesh: rows: 32 (over y, z), cols: 8 (over x, core).
Axes of the slice: x: 4, y: 4, z: 8, core: 2. Of those that a mesh axis runs over, the one named last changes fastest.
Arguments:
- features: bfloat16 [4, 256, 1280, 128], P(None, 'rows', 'cols'), may hold values from -60 to 60
- conv_first: bfloat16 [3, 3, 3, 128, 128], replicated, may hold values from -0.109375 to 0.109375
- first_reduce_kernel: bfloat16 [3, 3, 128, 256], replicated, may hold values from -0.1875 to 0.1875
- conv_second: bfloat16 [3, 3, 3, 256, 256], replicated, may hold values from -0.078125 to 0.078125
- second_reduce_kernel: bfloat16 [3, 3, 256, 512], replicated, may hold values from -0.125 to 0.125
- conv_last: bfloat16 [3, 3, 3, 512, 32], replicated, may hold values from -0.0546875 to 0.0546875
- gain_first: float32 [128], replicated, may hold values from 0.5 to 1.5
- shift_first: float32 [128], replicated, may hold values from -0.5 to 0.5
- gain_second: float32 [256], replicated, may hold values from 0.5 to 1.5
- shift_second: float32 [256], replicated, may hold values from -0.5 to 0.5
- gain_third: float32 [512], replicated, may hold values from 0.5 to 1.5
- shift_third: float32 [512], replicated, may hold values from -0.5 to 0.5
Outputs:
- moments: bfloat16 [4, 64, 320, 32], P(None, 'rows', 'cols')
All inputs are finite; a program needn't handle non-finite values.
Results may differ from a plain program's by a relative error of at most 0.01.
Values may be sent and summed in bfloat16 or wider, within the bound.
No kernel may reach another device: no remote copies, remote signals or barrier semaphores. Data moves between devices by JAX's collectives and lax.ppermute only.
A program may use at most 64 MiB of HBM per device.

v0:
```python
import jax
import jax.numpy as jnp
from jax import lax
from jax.sharding import Mesh
from jax.sharding import PartitionSpec as P

GROUPS = 32
ROWS_COLS = ("rows_0", "rows_1", "cols_0", "cols_1")
ROWS = ("rows_0", "rows_1")
COLS = ("cols_0", "cols_1")
epsilon = 1e-06


def shortened(array):
    return jax.tree.map(lambda a: a.astype(jnp.bfloat16) if a.dtype == jnp.float32 else a, array)


def extended_2(array, sides, width):
    for axis, dim in sides:
        peers, length = (lax.axis_size(axis), array.shape[dim])
        up = [(i, (i + 1) % peers) for i in range(peers - 1)]
        down = [(j, i) for i, j in up]
        last = lax.slice_in_dim(array, length - width, length, axis=dim)
        first = lax.slice_in_dim(array, 0, width, axis=dim)
        before = lax.ppermute(last, axis, up)
        after = lax.ppermute(first, axis, down)
        array = jnp.concatenate([before, array, after], axis=dim)
    return array


def one_axis_at_a_time(array, axes):
    for axis in axes:
        array = lax.psum(array, axis)
    return array


def dilated(input_video, weight_tables, strides):
    return lax.conv_general_dilated(
        input_video[None],
        weight_tables,
        strides,
        "VALID",
        dimension_numbers=("NDHWC", "DHWIO", "NDHWC"),
        preferred_element_type=jnp.float32,
    )[0]


def causal_conv(padding, weight_tables):
    widened = jnp.concatenate([padding[:1], padding[:1], padding], axis=0)
    return dilated(widened, weight_tables, (1, 1, 1))


def rimmed(input_video, margin):
    return extended_2(shortened(input_video), ((ROWS, 1), (COLS, 2)), margin).astype(
        input_video.dtype
    )


def moments(values, members):
    grouped = values.reshape(values.shape[:3] + (GROUPS, -1))
    summed, squares = (
        one_axis_at_a_time(jnp.sum(grouped, axis=(0, 1, 2, 4)), ROWS_COLS),
        one_axis_at_a_time(jnp.sum(jnp.square(grouped), axis=(0, 1, 2, 4)), ROWS_COLS),
    )
    mean_value = summed / members
    variance = jnp.maximum(squares / members - mean_value * mean_value, 0.0)
    return (mean_value, variance)


def activate(values, mean_value, variance, norm_gain, norm_shift):
    extent = values.shape
    grouped = values.reshape(extent[:3] + (GROUPS, -1))
    result = ((grouped - mean_value[:, None]) / jnp.sqrt(variance[:, None] + epsilon)).reshape(
        extent
    ) * norm_gain + norm_shift
    return jax.nn.silu(result).astype(jnp.bfloat16)


def group_members(frames, row_count, col_count, channels):
    return float(
        frames
        * row_count
        * col_count
        * lax.axis_size(ROWS)
        * lax.axis_size(COLS)
        * (channels // GROUPS)
    )


def encode_level(input_video, conv_weights, down_weights, norm_gain, norm_shift):
    frames, row_count, col_count = input_video.shape[:3]
    members = group_members(frames, row_count, col_count, conv_weights.shape[4])
    hidden = causal_conv(rimmed(input_video, 2)[:, 1:, 1:], conv_weights)
    mean_value, variance = moments(hidden[:, :row_count, :col_count], members)
    activated = activate(hidden, mean_value, variance, norm_gain, norm_shift)
    row_ids = lax.broadcasted_iota(jnp.int32, (1, row_count + 1, col_count + 1, 1), 1)
    col_ids = lax.broadcasted_iota(jnp.int32, (1, row_count + 1, col_count + 1, 1), 2)
    last_row = lax.axis_index(ROWS) == lax.axis_size(ROWS) - 1
    last_col = lax.axis_index(COLS) == lax.axis_size(COLS) - 1
    outside = (row_ids == row_count) & last_row | (col_ids == col_count) & last_col
    extended = jnp.where(outside, jnp.zeros((), jnp.bfloat16), activated)
    return dilated(extended, down_weights[None], (1, 2, 2)).astype(jnp.bfloat16)


def shards(
    features,
    conv_first,
    first_reduce_kernel,
    conv_second,
    second_reduce_kernel,
    conv_last,
    gain_first,
    shift_first,
    gain_second,
    shift_second,
    gain_third,
    shift_third,
):
    middle_level_features = encode_level(
        features, conv_first, first_reduce_kernel, gain_first, shift_first
    )
    coarsest_level_features = encode_level(
        middle_level_features, conv_second, second_reduce_kernel, gain_second, shift_second
    )
    frames, row_count, col_count, channels = coarsest_level_features.shape
    members = group_members(frames, row_count, col_count, channels)
    values = coarsest_level_features.astype(jnp.float32)
    mean_value, variance = moments(values, members)
    activated = activate(values, mean_value, variance, gain_third, shift_third)
    return causal_conv(rimmed(activated, 1), conv_last).astype(jnp.bfloat16)


def solution(mesh):
    split = Mesh(mesh.devices.reshape(4, 8, 4, 2), ("rows_0", "rows_1", "cols_0", "cols_1"))
    return jax.shard_map(
        shards,
        mesh=split,
        in_specs=(P(None, ROWS, COLS, None), P(), P(), P(), P(), P(), P(), P(), P(), P(), P(), P()),
        out_specs=P(None, ROWS, COLS, None),
        check_vma=False,
    )
```

profile of v0, /device:TPU:1, one launch (start us, length us, event | category | flops | bytes accessed | tf_op | source)
XLA Modules:
  0.0 256.2 jit_solution(17263411504774354062)
XLA Ops:
  0.0 2.1 fusion.93
  2.1 5.1 %collective-permute-start = (bf16[4,2,160,128]{3,2,1,0:T(8,128)(2,1)}, bf16[4,2,160,128]{3,2,1,0:T(8,128)(2,1)}, u32[]{:S(2)}, u32[]{:S(2)}) collective-permute-start(bf16[4,2,160,128]{3,2,1,0:T(8,128)(2,1)} %get-tuple-element.40), channel_id=1, source_target_pairs={{0,8},{8,16},{16,24},{24,32},{32,40},{40,48},{48,56},{56,64},{64,7... | collective-permute-start | bytes 983048 | tf_op jit(solution)/shard_map/ppermute | solution.py:25
  7.2 1.3 collective-permute-start.1
  8.5 4.6 %collective-permute-done = bf16[4,2,160,128]{3,2,1,0:T(8,128)(2,1)} collective-permute-done((bf16[4,2,160,128]{3,2,1,0:T(8,128)(2,1)}, bf16[4,2,160,128]{3,2,1,0:T(8,128)(2,1)}, u32[]{:S(2)}, u32[]{:S(2)}) %collective-permute-start) | collective-permute-done | bytes 327712 | tf_op jit(solution)/shard_map/ppermute | solution.py:25
  13.2 1.0 constant_dynamic-update-slice_fusion.2
  14.1 1.5 constant_dynamic-update-slice_fusion.1
  15.7 2.0 collective-permute-done.1
  17.7 1.0 constant_dynamic-update-slice_fusion
  18.7 4.9 %collective-permute-start.2 = (bf16[4,12,2,128]{3,2,1,0:T(2,128)(2,1)S(1)}, bf16[4,12,2,128]{3,2,1,0:T(2,128)(2,1)S(1)}, u32[]{:S(2)}, u32[]{:S(2)}) collective-permute-start(bf16[4,12,2,128]{3,2,1,0:T(2,128)(2,1)S(1)} %get-tuple-element.35), channel_id=1, source_target_pairs={{0,1},{1,2},{2,3},{3,4},{4,5},{5,6},{6,7},{8,9},{9,10},{10,11},{11... | collective-permute-start | bytes 73736 | tf_op jit(solution)/shard_map/ppermute | solution.py:25
  23.6 1.9 collective-permute-start.3
  26.2 2.5 collective-permute-done.3
  28.9 2.5 fusion.12
  31.4 1.8 pad
  33.2 5.7 %reshape.107 = bf16[6,11,1,8,21,128]{5,4,3,1,0,2:T(8,128)(2,1)} reshape(bf16[6,11,1,168,128]{4,3,1,0,2:T(8,128)(2,1)} %pad) | data formatting | bytes 5677056 | tf_op jit(solution)/shard_map/conv_general_dilated | solution.py:38
  39.0 2.4 copy.32
  41.6 11.6 %fusion.32 = f32[4,9,8,21,128]{4,2,3,1,0:T(8,128)S(1)} fusion(bf16[3,3,3,128,128]{4,3,2,1,0:T(8,128)(2,1)S(1)} %copy-done.10, bf16[6,11,1,7,2,128]{5,3,4,1,0,2:T(8,128)(2,1)S(1)} %slice.95, bf16[6,11,1,8,21,128]{5,3,4,1,0,2:T(8,128)(2,1)S(1)} %copy.32, pred[8,21]{0,1:T(8,128)(4,1)S(1)} %copy-done.13), kind=kOutput, calls=%fused_computation.45 | convolution fusion | flops 5360984064 | bytes 7056552 | tf_op jit(solution)/shard_map/conv_general_dilated | solution.py:38
  53.2 1.3 copy.33
  55.0 1.9 slice_reduce_fusion
  57.0 0.7 reduce_sum.70
  57.7 1.4 reduce_sum.76
  59.1 0.7 reduce_sum.74
  59.8 0.8 reduce_sum.77
  60.7 11.3 %all-reduce.8 = (f32[32]{0:T(128)S(1)}, f32[32]{0:T(128)S(1)}) all-reduce(f32[32]{0:T(128)S(1)} %reduce_sum.77, f32[32]{0:T(128)} %reduce_sum.74), channel_id=1, replica_groups=mesh['rows_0'=4,'rows_1'=8,'cols_0'=4,'cols_1'=2] {'rows_0'}, use_global_device_ids=true, to_apply=%region_8.0 | all-reduce | flops 64 | bytes 512 | tf_op jit(solution)/shard_map/psum | solution.py:33
  72.0 12.1 %all-reduce.2 = (f32[32]{0:T(128)S(1)}, f32[32]{0:T(128)S(1)}) all-reduce(f32[32]{0:T(128)S(1)} %get-tuple-element.27, f32[32]{0:T(128)S(1)} %get-tuple-element.28), channel_id=1, replica_groups=mesh['rows_0'=4,'rows_1'=8,'cols_0'=4,'cols_1'=2] {'rows_1'}, use_global_device_ids=true, to_apply=%region_9.0 | all-reduce | flops 64 | bytes 512 | tf_op jit(solution)/shard_map/psum | solution.py:33
  84.1 7.8 %all-reduce.5 = (f32[32]{0:T(128)S(1)}, f32[32]{0:T(128)}) all-reduce(f32[32]{0:T(128)S(1)} %get-tuple-element.15, f32[32]{0:T(128)S(1)} %get-tuple-element.16), channel_id=1, replica_groups=mesh['rows_0'=4,'rows_1'=8,'cols_0'=4,'cols_1'=2] {'cols_0'}, use_global_device_ids=true, to_apply=%region_10.11 | all-reduce | flops 64 | bytes 512 | tf_op jit(solution)/shard_map/psum | solution.py:33
  91.9 10.0 %all-reduce.11 = (f32[32]{0:T(128)S(1)}, f32[32]{0:T(128)S(1)}) all-reduce(f32[32]{0:T(128)S(1)} %get-tuple-element.21, f32[32]{0:T(128)} %get-tuple-element.22), channel_id=1, replica_groups=mesh['rows_0'=4,'rows_1'=8,'cols_0'=4,'cols_1'=2] {'cols_1'}, use_global_device_ids=true, to_apply=%region_11.12 | all-reduce | flops 64 | bytes 512 | tf_op jit(solution)/shard_map/psum | solution.py:33
  102.5 0.7 div.76
  103.2 0.7 sub.50
  104.5 2.9 %multiply_convert_fusion = bf16[4,9,8,21,128]{4,2,3,1,0:T(8,128)(2,1)S(1)} fusion(f32[4,9,8,21,128]{4,2,3,1,0:T(8,128)} %copy-done.2, f32[128]{0:T(128)} %param.19, f32[128]{0:T(128)} %param.18, f32[128]{0:T(128)} %div.76, f32[128]{0:T(128)} %sub.51), kind=kLoop, calls=%fused_computation.14 | loop fusion | flops 6967296 | bytes 4646912 | tf_op jit(solution)/shard_map/convert_element_type | solution.py:76
  108.1 2.3 slice_select_fusion
  111.3 0.8 copy-done.12
  112.1 1.1 select_convert_fusion
  114.2 2.0 collective-permute-start.4
  116.2 1.3 collective-permute-start.5
  117.5 5.4 %collective-permute-done.4 = bf16[4,2,80,256]{3,1,2,0:T(2,128)(2,1)S(1)} collective-permute-done((bf16[4,2,80,256]{3,1,2,0:T(2,128)(2,1)S(1)}, bf16[4,2,80,256]{3,1,2,0:T(2,128)(2,1)S(1)}, u32[]{:S(2)}, u32[]{:S(2)}) %collective-permute-start.4) | collective-permute-done | bytes 327712 | tf_op jit(solution)/shard_map/ppermute | solution.py:25
  122.9 3.8 %collective-permute-done.5 = bf16[4,2,80,256]{3,1,2,0:T(2,128)(2,1)S(1)} collective-permute-done((bf16[4,2,80,256]{3,1,2,0:T(2,128)(2,1)S(1)}, bf16[4,2,80,256]{3,1,2,0:T(2,128)(2,1)S(1)}, u32[]{:S(2)}, u32[]{:S(2)}) %collective-permute-start.5) | collective-permute-done | bytes 327712 | tf_op jit(solution)/shard_map/ppermute | solution.py:26
  126.8 2.6 %collective-permute-start.6 = (bf16[4,8,2,256]{3,1,2,0:T(8,128)(2,1)S(1)}, bf16[4,8,2,256]{3,1,2,0:T(8,128)(2,1)S(1)}, u32[]{:S(2)}, u32[]{:S(2)}) collective-permute-start(bf16[4,8,2,256]{3,1,2,0:T(8,128)(2,1)S(1)} %get-tuple-element.37), channel_id=1, source_target_pairs={{0,1},{1,2},{2,3},{3,4},{4,5},{5,6},{6,7},{8,9},{9,10},{10,11},{11... | collective-permute-start | bytes 98312 | tf_op jit(solution)/shard_map/ppermute | solution.py:25
  129.4 2.1 collective-permute-start.7
  131.6 3.1 %collective-permute-done.7 = bf16[4,8,2,256]{3,1,2,0:T(8,128)(2,1)S(1)} collective-permute-done((bf16[4,8,2,256]{3,1,2,0:T(8,128)(2,1)S(1)}, bf16[4,8,2,256]{3,1,2,0:T(8,128)(2,1)S(1)}, u32[]{:S(2)}, u32[]{:S(2)}) %collective-permute-start.7) | collective-permute-done | bytes 32800 | tf_op jit(solution)/shard_map/ppermute | solution.py:26
  135.0 1.7 fusion.24
  137.8 7.3 %fusion.43 = f32[4,5,8,11,256]{4,2,3,1,0:T(8,128)S(1)} fusion(bf16[3,3,3,256,256]{4,3,2,1,0:T(8,128)(2,1)S(1)} %copy-done, bf16[6,7,1,7,2,256]{5,3,4,1,0,2:T(8,128)(2,1)S(1)} %slice.103, bf16[6,7,1,8,11,256]{5,3,4,1,0,2:T(8,128)(2,1)S(1)} %copy.39, pred[8,11]{0,1:T(8,128)(4,1)S(1)} %copy-done.14), kind=kOutput, calls=%fused_computation.55 | convolution fusion | flops 6235701248 | bytes 7534680 | tf_op jit(solution)/shard_map/conv_general_dilated | solution.py:38
  145.1 0.7 copy.40
  147.2 7.9 %all-reduce.7 = (f32[32]{0:T(128)S(1)}, f32[32]{0:T(128)S(1)}) all-reduce(f32[32]{0:T(128)S(1)} %reduce_sum.89, f32[32]{0:T(128)S(1)} %reduce_sum.83), channel_id=1, replica_groups=mesh['rows_0'=4,'rows_1'=8,'cols_0'=4,'cols_1'=2] {'rows_0'}, use_global_device_ids=true, to_apply=%region_20.21 | all-reduce | flops 64 | bytes 512 | tf_op jit(solution)/shard_map/psum | solution.py:33
  155.1 13.8 %all-reduce.1 = (f32[32]{0:T(128)S(1)}, f32[32]{0:T(128)S(1)}) all-reduce(f32[32]{0:T(128)S(1)} %get-tuple-element.25, f32[32]{0:T(128)S(1)} %get-tuple-element.26), channel_id=1, replica_groups=mesh['rows_0'=4,'rows_1'=8,'cols_0'=4,'cols_1'=2] {'rows_1'}, use_global_device_ids=true, to_apply=%region_21.22 | all-reduce | flops 64 | bytes 512 | tf_op jit(solution)/shard_map/psum | solution.py:33
  168.9 6.9 %all-reduce.4 = (f32[32]{0:T(128)S(1)}, f32[32]{0:T(128)S(1)}) all-reduce(f32[32]{0:T(128)S(1)} %get-tuple-element.13, f32[32]{0:T(128)S(1)} %get-tuple-element.14), channel_id=1, replica_groups=mesh['rows_0'=4,'rows_1'=8,'cols_0'=4,'cols_1'=2] {'cols_0'}, use_global_device_ids=true, to_apply=%region_22.23 | all-reduce | flops 64 | bytes 512 | tf_op jit(solution)/shard_map/psum | solution.py:33
  175.8 9.0 %all-reduce.10 = (f32[32]{0:T(128)S(1)}, f32[32]{0:T(128)S(1)}) all-reduce(f32[32]{0:T(128)S(1)} %get-tuple-element.19, f32[32]{0:T(128)S(1)} %get-tuple-element.20), channel_id=1, replica_groups=mesh['rows_0'=4,'rows_1'=8,'cols_0'=4,'cols_1'=2] {'cols_1'}, use_global_device_ids=true, to_apply=%region_23.24 | all-reduce | flops 64 | bytes 512 | tf_op jit(solution)/shard_map/psum | solution.py:33
  185.2 2.1 multiply_convert_fusion.1
  187.6 1.1 slice_select_fusion.1
  189.4 0.9 copy-done.9
  190.4 1.2 fusion.68
  192.0 7.7 %all-reduce.6 = (f32[32]{0:T(128)S(1)}, f32[32]{0:T(128)S(1)}) all-reduce(f32[32]{0:T(128)S(1)} %reduce_sum.113, f32[32]{0:T(128)S(1)} %reduce_sum.110), channel_id=1, replica_groups=mesh['rows_0'=4,'rows_1'=8,'cols_0'=4,'cols_1'=2] {'rows_0'}, use_global_device_ids=true, to_apply=%region_32.33 | all-reduce | flops 64 | bytes 512 | tf_op jit(solution)/shard_map/psum | solution.py:33
  199.7 10.7 %all-reduce = (f32[32]{0:T(128)S(1)}, f32[32]{0:T(128)S(1)}) all-reduce(f32[32]{0:T(128)S(1)} %get-tuple-element.23, f32[32]{0:T(128)S(1)} %get-tuple-element.24), channel_id=1, replica_groups=mesh['rows_0'=4,'rows_1'=8,'cols_0'=4,'cols_1'=2] {'rows_1'}, use_global_device_ids=true, to_apply=%region_33.34 | all-reduce | flops 64 | bytes 512 | tf_op jit(solution)/shard_map/psum | solution.py:33
  210.3 6.1 %all-reduce.3 = (f32[32]{0:T(128)S(1)}, f32[32]{0:T(128)S(1)}) all-reduce(f32[32]{0:T(128)S(1)} %get-tuple-element.11, f32[32]{0:T(128)S(1)} %get-tuple-element.12), channel_id=1, replica_groups=mesh['rows_0'=4,'rows_1'=8,'cols_0'=4,'cols_1'=2] {'cols_0'}, use_global_device_ids=true, to_apply=%region_34.35 | all-reduce | flops 64 | bytes 512 | tf_op jit(solution)/shard_map/psum | solution.py:33
  216.5 10.0 %all-reduce.9 = (f32[32]{0:T(128)S(1)}, f32[32]{0:T(128)S(1)}) all-reduce(f32[32]{0:T(128)S(1)} %get-tuple-element.17, f32[32]{0:T(128)S(1)} %get-tuple-element.18), channel_id=1, replica_groups=mesh['rows_0'=4,'rows_1'=8,'cols_0'=4,'cols_1'=2] {'cols_1'}, use_global_device_ids=true, to_apply=%region_35.36 | all-reduce | flops 64 | bytes 512 | tf_op jit(solution)/shard_map/psum | solution.py:33
  227.7 3.6 %collective-permute-start.8 = (bf16[4,1,40,512]{3,2,1,0:T(8,128)(2,1)S(1)}, bf16[4,1,40,512]{3,2,1,0:T(8,128)(2,1)S(1)}, u32[]{:S(2)}, u32[]{:S(2)}) collective-permute-start(bf16[4,1,40,512]{3,2,1,0:T(8,128)(2,1)S(1)} %get-tuple-element.45), channel_id=1, source_target_pairs={{0,8},{8,16},{16,24},{24,32},{32,40},{40,48},{48,56},{56,64},{64,7... | collective-permute-start | bytes 491528 | tf_op jit(solution)/shard_map/ppermute | solution.py:25
  231.4 1.3 collective-permute-start.9
  232.7 1.9 collective-permute-done.8
  234.6 3.8 %collective-permute-done.9 = bf16[4,1,40,512]{3,2,1,0:T(8,128)(2,1)S(1)} collective-permute-done((bf16[4,1,40,512]{3,2,1,0:T(8,128)(2,1)S(1)}, bf16[4,1,40,512]{3,2,1,0:T(8,128)(2,1)S(1)}, u32[]{:S(2)}, u32[]{:S(2)}) %collective-permute-start.9) | collective-permute-done | bytes 163872 | tf_op jit(solution)/shard_map/ppermute | solution.py:26
  238.4 4.6 %collective-permute-start.10 = (bf16[4,4,1,512]{3,2,1,0:T(2,128)(2,1)S(1)}, bf16[4,4,1,512]{3,2,1,0:T(2,128)(2,1)S(1)}, u32[]{:S(2)}, u32[]{:S(2)}) collective-permute-start(bf16[4,4,1,512]{3,2,1,0:T(2,128)(2,1)S(1)} %get-tuple-element.41), channel_id=1, source_target_pairs={{0,1},{1,2},{2,3},{3,4},{4,5},{5,6},{6,7},{8,9},{9,10},{10,11},{11... | collective-permute-start | bytes 49160 | tf_op jit(solution)/shard_map/ppermute | solution.py:25
  243.0 1.9 collective-permute-start.11
  245.0 3.3 %collective-permute-done.11 = bf16[4,4,1,512]{3,2,1,0:T(2,128)(2,1)S(1)} collective-permute-done((bf16[4,4,1,512]{3,2,1,0:T(2,128)(2,1)S(1)}, bf16[4,4,1,512]{3,2,1,0:T(2,128)(2,1)S(1)}, u32[]{:S(2)}, u32[]{:S(2)}) %collective-permute-start.11) | collective-permute-done | bytes 16416 | tf_op jit(solution)/shard_map/ppermute | solution.py:26
  248.7 0.8 copy.52
  250.7 2.9 %fusion.63 = bf16[4,2,8,6,32]{4,2,3,1,0:T(8,128)(2,1)S(1)} fusion(bf16[3,3,3,512,32]{3,4,2,1,0:T(8,128)(2,1)S(1)} %copy-done.11, bf16[6,4,1,7,2,512]{5,3,4,1,0,2:T(8,128)(2,1)S(1)} %slice.111, bf16[6,4,1,8,6,512]{5,3,4,1,0,2:T(8,128)(2,1)S(1)} %copy.48, pred[8,6]{0,1:T(8,128)(4,1)S(1)} %copy-done.16), kind=kOutput, calls=%fused_computation.68 | convolution fusion | flops 344481792 | bytes 2433072 | tf_op jit(solution)/shard_map/conv_general_dilated | solution.py:38
  254.4 1.6 copy.50
  (96 shorter events, 13.5 us)
Async XLA Ops:
  0.0 137.6 %copy-start = (bf16[3,3,3,256,256]{4,3,2,1,0:T(8,128)(2,1)S(1)}, bf16[3,3,3,256,256]{4,3,2,1,0:T(8,128)(2,1)}, u32[]{:S(2)}) copy-start(bf16[3,3,3,256,256]{4,3,2,1,0:T(8,128)(2,1)} %param.15) | copy-start | bytes 10616836
  2.1 11.0 %collective-permute-start = (bf16[4,2,160,128]{3,2,1,0:T(8,128)(2,1)}, bf16[4,2,160,128]{3,2,1,0:T(8,128)(2,1)}, u32[]{:S(2)}, u32[]{:S(2)}) collective-permute-start(bf16[4,2,160,128]{3,2,1,0:T(8,128)(2,1)} %get-tuple-element.40), channel_id=1, source_target_pairs={{0,8},{8,16},{16,24},{24,32},{32,40},{40,48},{48,56},{56,64},{64,7... | collective-permute-start | bytes 983048 | tf_op jit(solution)/shard_map/ppermute | solution.py:25
  7.2 10.5 %collective-permute-start.1 = (bf16[4,2,160,128]{3,2,1,0:T(8,128)(2,1)}, bf16[4,2,160,128]{3,2,1,0:T(8,128)(2,1)}, u32[]{:S(2)}, u32[]{:S(2)}) collective-permute-start(bf16[4,2,160,128]{3,2,1,0:T(8,128)(2,1)} %get-tuple-element.39), channel_id=1, source_target_pairs={{8,0},{16,8},{24,16},{32,24},{40,32},{48,40},{56,48},{64,56},{72,6... | collective-permute-start | bytes 983048 | tf_op jit(solution)/shard_map/ppermute | solution.py:26
  18.7 7.5 %collective-permute-start.2 = (bf16[4,12,2,128]{3,2,1,0:T(2,128)(2,1)S(1)}, bf16[4,12,2,128]{3,2,1,0:T(2,128)(2,1)S(1)}, u32[]{:S(2)}, u32[]{:S(2)}) collective-permute-start(bf16[4,12,2,128]{3,2,1,0:T(2,128)(2,1)S(1)} %get-tuple-element.35), channel_id=1, source_target_pairs={{0,1},{1,2},{2,3},{3,4},{4,5},{5,6},{6,7},{8,9},{9,10},{10,11},{11... | collective-permute-start | bytes 73736 | tf_op jit(solution)/shard_map/ppermute | solution.py:25
  23.6 5.1 %collective-permute-start.3 = (bf16[4,12,2,128]{3,2,1,0:T(2,128)(2,1)S(1)}, bf16[4,12,2,128]{3,2,1,0:T(2,128)(2,1)S(1)}, u32[]{:S(2)}, u32[]{:S(2)}) collective-permute-start(bf16[4,12,2,128]{3,2,1,0:T(2,128)(2,1)S(1)} %get-tuple-element.36), channel_id=1, source_target_pairs={{1,0},{2,1},{3,2},{4,3},{5,4},{6,5},{7,6},{9,8},{10,9},{11,10},{12... | collective-permute-start | bytes 73736 | tf_op jit(solution)/shard_map/ppermute | solution.py:26
  39.0 2.6 copy-start.10
  39.0 2.6 copy-start.13
  53.2 1.6 copy-start.2
  107.4 0.7 copy-start.4
  111.0 1.1 copy-start.12
  111.0 1.1 copy-start.15
  114.2 8.7 %collective-permute-start.4 = (bf16[4,2,80,256]{3,1,2,0:T(2,128)(2,1)S(1)}, bf16[4,2,80,256]{3,1,2,0:T(2,128)(2,1)S(1)}, u32[]{:S(2)}, u32[]{:S(2)}) collective-permute-start(bf16[4,2,80,256]{3,1,2,0:T(2,128)(2,1)S(1)} %get-tuple-element.43), channel_id=1, source_target_pairs={{0,8},{8,16},{16,24},{24,32},{32,40},{40,48},{48,56},{56,64},{64,7... | collective-permute-start | bytes 983048 | tf_op jit(solution)/shard_map/ppermute | solution.py:25
  116.2 10.5 %collective-permute-start.5 = (bf16[4,2,80,256]{3,1,2,0:T(2,128)(2,1)S(1)}, bf16[4,2,80,256]{3,1,2,0:T(2,128)(2,1)S(1)}, u32[]{:S(2)}, u32[]{:S(2)}) collective-permute-start(bf16[4,2,80,256]{3,1,2,0:T(2,128)(2,1)S(1)} %get-tuple-element.44), channel_id=1, source_target_pairs={{8,0},{16,8},{24,16},{32,24},{40,32},{48,40},{56,48},{64,56},{72,6... | collective-permute-start | bytes 983048 | tf_op jit(solution)/shard_map/ppermute | solution.py:26
  126.8 4.8 %collective-permute-start.6 = (bf16[4,8,2,256]{3,1,2,0:T(8,128)(2,1)S(1)}, bf16[4,8,2,256]{3,1,2,0:T(8,128)(2,1)S(1)}, u32[]{:S(2)}, u32[]{:S(2)}) collective-permute-start(bf16[4,8,2,256]{3,1,2,0:T(8,128)(2,1)S(1)} %get-tuple-element.37), channel_id=1, source_target_pairs={{0,1},{1,2},{2,3},{3,4},{4,5},{5,6},{6,7},{8,9},{9,10},{10,11},{11... | collective-permute-start | bytes 98312 | tf_op jit(solution)/shard_map/ppermute | solution.py:25
  129.4 5.2 %collective-permute-start.7 = (bf16[4,8,2,256]{3,1,2,0:T(8,128)(2,1)S(1)}, bf16[4,8,2,256]{3,1,2,0:T(8,128)(2,1)S(1)}, u32[]{:S(2)}, u32[]{:S(2)}) collective-permute-start(bf16[4,8,2,256]{3,1,2,0:T(8,128)(2,1)S(1)} %get-tuple-element.38), channel_id=1, source_target_pairs={{1,0},{2,1},{3,2},{4,3},{5,4},{6,5},{7,6},{9,8},{10,9},{11,10},{12... | collective-permute-start | bytes 98312 | tf_op jit(solution)/shard_map/ppermute | solution.py:26
  137.1 0.7 copy-start.14
  145.0 1.2 copy-start.3
  145.8 39.4 %copy-start.7 = (f32[256]{0:T(256)S(1)}, f32[256]{0:T(256)}, u32[]{:S(2)}) copy-start(f32[256]{0:T(256)} %param.21) | copy-start | bytes 3076
  145.8 39.4 %copy-start.8 = (f32[256]{0:T(256)S(1)}, f32[256]{0:T(256)}, u32[]{:S(2)}) copy-start(f32[256]{0:T(256)} %param.20) | copy-start | bytes 3076
  188.7 1.7 copy-start.9
  188.7 1.7 copy-start.16
  190.4 37.1 %copy-start.5 = (f32[512]{0:T(512)S(1)}, f32[512]{0:T(512)}, u32[]{:S(2)}) copy-start(f32[512]{0:T(512)} %param.23) | copy-start | bytes 6148
  190.4 37.1 %copy-start.6 = (f32[512]{0:T(512)S(1)}, f32[512]{0:T(512)}, u32[]{:S(2)}) copy-start(f32[512]{0:T(512)} %param.22) | copy-start | bytes 6148
  227.7 6.9 %collective-permute-start.8 = (bf16[4,1,40,512]{3,2,1,0:T(8,128)(2,1)S(1)}, bf16[4,1,40,512]{3,2,1,0:T(8,128)(2,1)S(1)}, u32[]{:S(2)}, u32[]{:S(2)}) collective-permute-start(bf16[4,1,40,512]{3,2,1,0:T(8,128)(2,1)S(1)} %get-tuple-element.45), channel_id=1, source_target_pairs={{0,8},{8,16},{16,24},{24,32},{32,40},{40,48},{48,56},{56,64},{64,7... | collective-permute-start | bytes 491528 | tf_op jit(solution)/shard_map/ppermute | solution.py:25
  231.4 7.0 %collective-permute-start.9 = (bf16[4,1,40,512]{3,2,1,0:T(8,128)(2,1)S(1)}, bf16[4,1,40,512]{3,2,1,0:T(8,128)(2,1)S(1)}, u32[]{:S(2)}, u32[]{:S(2)}) collective-permute-start(bf16[4,1,40,512]{3,2,1,0:T(8,128)(2,1)S(1)} %get-tuple-element.46), channel_id=1, source_target_pairs={{8,0},{16,8},{24,16},{32,24},{40,32},{48,40},{56,48},{64,56},{72,6... | collective-permute-start | bytes 491528 | tf_op jit(solution)/shard_map/ppermute | solution.py:26
  238.4 6.5 %collective-permute-start.10 = (bf16[4,4,1,512]{3,2,1,0:T(2,128)(2,1)S(1)}, bf16[4,4,1,512]{3,2,1,0:T(2,128)(2,1)S(1)}, u32[]{:S(2)}, u32[]{:S(2)}) collective-permute-start(bf16[4,4,1,512]{3,2,1,0:T(2,128)(2,1)S(1)} %get-tuple-element.41), channel_id=1, source_target_pairs={{0,1},{1,2},{2,3},{3,4},{4,5},{5,6},{6,7},{8,9},{9,10},{10,11},{11... | collective-permute-start | bytes 49160 | tf_op jit(solution)/shard_map/ppermute | solution.py:25
  243.0 5.2 %collective-permute-start.11 = (bf16[4,4,1,512]{3,2,1,0:T(2,128)(2,1)S(1)}, bf16[4,4,1,512]{3,2,1,0:T(2,128)(2,1)S(1)}, u32[]{:S(2)}, u32[]{:S(2)}) collective-permute-start(bf16[4,4,1,512]{3,2,1,0:T(2,128)(2,1)S(1)} %get-tuple-element.42), channel_id=1, source_target_pairs={{1,0},{2,1},{3,2},{4,3},{5,4},{6,5},{7,6},{9,8},{10,9},{11,10},{12... | collective-permute-start | bytes 49160 | tf_op jit(solution)/shard_map/ppermute | solution.py:26
  249.5 1.2 copy-start.11
  250.7 5.3 %copy-start.1 = (bf16[3,3,3,256,256]{4,3,2,1,0:T(8,128)(2,1)S(1)}, bf16[3,3,3,256,256]{4,3,2,1,0:T(8,128)(2,1)}, u32[]{:S(2)}) copy-start(bf16[3,3,3,256,256]{4,3,2,1,0:T(8,128)(2,1)} %param.15) | copy-start | bytes 10616836
where the time goes:
time: 260 us; the launch traced here: 256 us
  blocking collectives  113 us (43%)
  local copies, waits for them, and re-layouts  35.3 us (14%)
  starting transfers between devices  32.6 us (13%)
  waiting for transfers between devices  30.5 us (12%)
  matrix products  24.1 us (9%)
  other arithmetic  19.6 us (8%)
    psum x12, blocking collectives, one_axis_at_a_time(): array = lax.psum(array, axis)  113 us
    conv_general_dilated x5, matrix products, dilated(): lax.conv_general_dilated(input_video[None], weight_tables, strides, 'VALI...  24.1 us
    ppermute x6, starting transfers between devices, extended_2(): before = lax.ppermute(last, axis, up)  22.8 us
    ppermute x6, waiting for transfers between devices, extended_2(): after = lax.ppermute(first, axis, down)  18.5 us
    ppermute x6, waiting for transfers between devices, extended_2(): before = lax.ppermute(last, axis, up)  11.9 us
    conv_general_dilated x13, local copies, waits for them, and re-layouts, dilated(): lax.conv_general_dilated(input_video[None], weight_tables, strides, 'VALI...  11.9 us
    ppermute x6, starting transfers between devices, extended_2(): after = lax.ppermute(first, axis, down)  9.77 us
    unnamed x37, local copies, waits for them, and re-layouts  6.04 us
  transfers between devices with their start and end apart: 12, of which 9 were waited for; matrix products, arithmetic and copies ran while one was open for 1% of the time, Pallas kernels for 0%

commit v1 on v0

--- a/solution.py
+++ b/solution.py
@@ -30,7 +30,7 @@
 
 def one_axis_at_a_time(array, axes):
     for axis in axes:
-        array = lax.psum(array, axis)
+        array = jnp.sum(lax.all_gather(array, axis), axis=0)
     return array
 
 

time: 260 us -> 280 us (1.077)
  local copies, waits for them, and re-layouts: 35.3 us -> 50.9 us
  waiting for transfers between devices: 30.5 us -> 27.7 us
    unnamed x0 -> x12, blocking collectives: none -> 115 us
    psum x12 -> x0, blocking collectives: 113 us -> none  [one_axis_at_a_time(): array = lax.psum(array, axis)]
    unnamed x37 -> x101, local copies, waits for them, and re-layouts: 6.04 us -> 19.5 us
  transfers between devices with their start and end apart: 12 -> 12, of which waited for: 9 -> 8; matrix products, arithmetic and copies ran while one was open for 1% -> 2% of each run, Pallas kernels for 0% -> 0%
where the time goes in v1:
time: 280 us; the launch traced here: 276 us
  blocking collectives  115 us (41%)
  local copies, waits for them, and re-layouts  50.9 us (18%)
  starting transfers between devices  33 us (12%)
  waiting for transfers between devices  27.7 us (10%)
  matrix products  24.1 us (9%)
  other arithmetic  21.8 us (8%)
  between operations  3.54 us (1%)
    unnamed x12, blocking collectives  115 us
    conv_general_dilated x5, matrix products, dilated(): lax.conv_general_dilated(input_video[None], weight_tables, strides, 'VALI...  24.1 us
    ppermute x6, starting transfers between devices, extended_2(): before = lax.ppermute(last, axis, up)  23 us
    unnamed x101, local copies, waits for them, and re-layouts  19.5 us
    ppermute x6, waiting for transfers between devices, extended_2(): after = lax.ppermute(first, axis, down)  15.8 us
    ppermute x6, waiting for transfers between devices, extended_2(): before = lax.ppermute(last, axis, up)  11.9 us
    conv_general_dilated x13, local copies, waits for them, and re-layouts, dilated(): lax.conv_general_dilated(input_video[None], weight_tables, strides, 'VALI...  11.4 us
    ppermute x6, starting transfers between devices, extended_2(): after = lax.ppermute(first, axis, down)  9.99 us
  transfers between devices with their start and end apart: 12, of which 8 were waited for; matrix products, arithmetic and copies ran while one was open for 2% of the time, Pallas kernels for 0%

profile of v1, /device:TPU:1, one launch (start us, length us, event | category | flops | bytes accessed | tf_op | source)
XLA Modules:
  0.0 275.6 jit_solution(2511749912499371518)
XLA Ops:
  0.0 2.1 fusion.93
  2.1 5.2 %collective-permute-start = (bf16[4,2,160,128]{3,2,1,0:T(8,128)(2,1)}, bf16[4,2,160,128]{3,2,1,0:T(8,128)(2,1)}, u32[]{:S(2)}, u32[]{:S(2)}) collective-permute-start(bf16[4,2,160,128]{3,2,1,0:T(8,128)(2,1)} %get-tuple-element.40), channel_id=1, source_target_pairs={{0,8},{8,16},{16,24},{24,32},{32,40},{40,48},{48,56},{56,64},{64,7... | collective-permute-start | bytes 983048 | tf_op jit(solution)/shard_map/ppermute | solution.py:25
  7.4 1.3 collective-permute-start.1
  8.7 4.6 %collective-permute-done = bf16[4,2,160,128]{3,2,1,0:T(8,128)(2,1)} collective-permute-done((bf16[4,2,160,128]{3,2,1,0:T(8,128)(2,1)}, bf16[4,2,160,128]{3,2,1,0:T(8,128)(2,1)}, u32[]{:S(2)}, u32[]{:S(2)}) %collective-permute-start) | collective-permute-done | bytes 327712 | tf_op jit(solution)/shard_map/ppermute | solution.py:25
  13.3 1.0 constant_dynamic-update-slice_fusion.2
  14.3 1.5 constant_dynamic-update-slice_fusion.1
  15.8 2.0 collective-permute-done.1
  17.8 1.0 constant_dynamic-update-slice_fusion
  18.9 1.3 copy-done.3
  20.8 4.9 %collective-permute-start.2 = (bf16[4,12,2,128]{3,2,1,0:T(2,128)(2,1)}, bf16[4,12,2,128]{3,2,1,0:T(2,128)(2,1)}, u32[]{:S(2)}, u32[]{:S(2)}) collective-permute-start(bf16[4,12,2,128]{3,2,1,0:T(2,128)(2,1)} %get-tuple-element.35), channel_id=1, source_target_pairs={{0,1},{1,2},{2,3},{3,4},{4,5},{5,6},{6,7},{8,9},{9,10},{10,11},{11... | collective-permute-start | bytes 73736 | tf_op jit(solution)/shard_map/ppermute | solution.py:25
  25.7 1.9 collective-permute-start.3
  33.2 1.2 pad_maximum_fusion.6
  34.4 3.2 %fusion.12 = bf16[6,11,1,163,128]{4,3,1,0,2:T(8,128)(2,1)S(1)} fusion(bf16[4,12,2,128]{3,2,1,0:T(2,128)(2,1)} %collective-permute-done.3, bf16[4,12,160,128]{3,2,1,0:T(8,128)(2,1)S(1)} %copy-done.4, bf16[4,12,2,128]{3,2,1,0:T(2,128)(2,1)} %collective-permute-done.2, bf16[1,11,163,128]{3,2,1,0:T(8,128)(2,1)S(1)} %pad_maximum_fusion.6), kind=kLoop, calls=%fused_computation.18 | loop fusion | flops 13770240 | bytes 5228288 | tf_op jit(solution)/shard_map/broadcast_in_dim | solution.py:39
  37.6 1.8 pad
  39.4 5.6 %reshape.143 = bf16[6,11,1,8,21,128]{5,4,3,1,0,2:T(8,128)(2,1)} reshape(bf16[6,11,1,168,128]{4,3,1,0,2:T(8,128)(2,1)} %pad) | data formatting | bytes 5677056 | tf_op jit(solution)/shard_map/conv_general_dilated | solution.py:38
  45.1 2.4 copy.50
  47.6 11.6 %fusion.32 = f32[4,9,8,21,128]{4,2,3,1,0:T(8,128)S(1)} fusion(bf16[3,3,3,128,128]{4,3,2,1,0:T(8,128)(2,1)S(1)} %copy-done.12, bf16[6,11,1,7,2,128]{5,3,4,1,0,2:T(8,128)(2,1)S(1)} %slice.95, bf16[6,11,1,8,21,128]{5,3,4,1,0,2:T(8,128)(2,1)S(1)} %copy.50, pred[8,21]{0,1:T(8,128)(4,1)S(1)} %copy-done.19), kind=kOutput, calls=%fused_computation.45 | convolution fusion | flops 5360984064 | bytes 7056552 | tf_op jit(solution)/shard_map/conv_general_dilated | solution.py:38
  59.3 1.0 copy.51
  61.1 1.9 slice_reduce_fusion
  63.1 0.7 reduce_sum.313
  63.8 1.4 reduce_sum.320
  65.9 0.8 reduce_sum.321
  66.8 0.9 dynamic-update-slice
  68.2 1.3 dynamic-update-slice.4
  69.4 11.4 %all-reduce.32 = (f32[128]{0:T(128)S(1)}, f32[128]{0:T(128)S(1)}) all-reduce(f32[128]{0:T(128)} %dynamic-update-slice.4, f32[128]{0:T(128)S(1)} %dynamic-update-slice), channel_id=6, replica_groups=mesh['rows_0'=4,'rows_1'=8,'cols_0'=4,'cols_1'=2] {'rows_0'}, use_global_device_ids=true, to_apply=%add.4 | all-reduce | flops 256 | bytes 2048
  81.5 12.0 %all-reduce.26 = (f32[256]{0:T(256)S(1)}, f32[256]{0:T(256)S(1)}) all-reduce(f32[256]{0:T(256)S(1)} %dynamic-update-slice.5, f32[256]{0:T(256)S(1)} %dynamic-update-slice.1), channel_id=7, replica_groups=mesh['rows_0'=4,'rows_1'=8,'cols_0'=4,'cols_1'=2] {'rows_1'}, use_global_device_ids=true, to_apply=%add.5 | all-reduce | flops 512 | bytes 4096
  94.4 1.3 dynamic-update-slice.6
  95.7 8.2 %all-reduce.29 = (f32[128]{0:T(128)S(1)}, f32[128]{0:T(128)S(1)}) all-reduce(f32[128]{0:T(128)} %dynamic-update-slice.6, f32[128]{0:T(128)S(1)} %dynamic-update-slice.2), channel_id=8, replica_groups=mesh['rows_0'=4,'rows_1'=8,'cols_0'=4,'cols_1'=2] {'cols_0'}, use_global_device_ids=true, to_apply=%add.6 | all-reduce | flops 256 | bytes 2048
  104.5 10.9 %all-reduce.35 = (f32[64]{0:T(128)S(1)}, f32[64]{0:T(128)S(1)}) all-reduce(f32[64]{0:T(128)S(1)} %dynamic-update-slice.7, f32[64]{0:T(128)S(1)} %dynamic-update-slice.3), channel_id=9, replica_groups=mesh['rows_0'=4,'rows_1'=8,'cols_0'=4,'cols_1'=2] {'cols_1'}, use_global_device_ids=true, to_apply=%add.7 | all-reduce | flops 128 | bytes 1024
  118.3 2.9 %multiply_convert_fusion = bf16[4,9,8,21,128]{4,2,3,1,0:T(8,128)(2,1)S(1)} fusion(f32[4,9,8,21,128]{4,2,3,1,0:T(8,128)} %copy-done.2, f32[128]{0:T(128)} %param.19, f32[128]{0:T(128)} %param.18, f32[128]{0:T(128)} %div.76, f32[128]{0:T(128)} %sub.66), kind=kLoop, calls=%fused_computation.14 | loop fusion | flops 6967296 | bytes 4646912 | tf_op jit(solution)/shard_map/convert_element_type | solution.py:76
  121.9 2.3 slice_select_fusion
  125.1 0.8 copy-done.14
  125.9 1.1 select_convert_fusion
  128.0 2.0 collective-permute-start.4
  130.0 1.3 collective-permute-start.5
  131.3 5.4 %collective-permute-done.4 = bf16[4,2,80,256]{3,1,2,0:T(2,128)(2,1)S(1)} collective-permute-done((bf16[4,2,80,256]{3,1,2,0:T(2,128)(2,1)S(1)}, bf16[4,2,80,256]{3,1,2,0:T(2,128)(2,1)S(1)}, u32[]{:S(2)}, u32[]{:S(2)}) %collective-permute-start.4) | collective-permute-done | bytes 327712 | tf_op jit(solution)/shard_map/ppermute | solution.py:25
  136.7 3.8 %collective-permute-done.5 = bf16[4,2,80,256]{3,1,2,0:T(2,128)(2,1)S(1)} collective-permute-done((bf16[4,2,80,256]{3,1,2,0:T(2,128)(2,1)S(1)}, bf16[4,2,80,256]{3,1,2,0:T(2,128)(2,1)S(1)}, u32[]{:S(2)}, u32[]{:S(2)}) %collective-permute-start.5) | collective-permute-done | bytes 327712 | tf_op jit(solution)/shard_map/ppermute | solution.py:26
  140.6 2.6 collective-permute-start.6
  143.2 2.1 collective-permute-start.7
  145.4 3.1 %collective-permute-done.7 = bf16[4,8,2,256]{3,1,2,0:T(8,128)(2,1)S(1)} collective-permute-done((bf16[4,8,2,256]{3,1,2,0:T(8,128)(2,1)S(1)}, bf16[4,8,2,256]{3,1,2,0:T(8,128)(2,1)S(1)}, u32[]{:S(2)}, u32[]{:S(2)}) %collective-permute-start.7) | collective-permute-done | bytes 32800 | tf_op jit(solution)/shard_map/ppermute | solution.py:26
  148.8 1.9 fusion.24
  151.8 7.3 %fusion.43 = f32[4,5,8,11,256]{4,2,3,1,0:T(8,128)S(1)} fusion(bf16[3,3,3,256,256]{4,3,2,1,0:T(8,128)(2,1)S(1)} %copy-done, bf16[6,7,1,7,2,256]{5,3,4,1,0,2:T(8,128)(2,1)S(1)} %slice.103, bf16[6,7,1,8,11,256]{5,3,4,1,0,2:T(8,128)(2,1)S(1)} %copy.57, pred[8,11]{0,1:T(8,128)(4,1)S(1)} %copy-done.20), kind=kOutput, calls=%fused_computation.55 | convolution fusion | flops 6235701248 | bytes 7534680 | tf_op jit(solution)/shard_map/conv_general_dilated | solution.py:38
  161.7 7.9 %all-reduce.31 = (f32[128]{0:T(128)S(1)}, f32[128]{0:T(128)S(1)}) all-reduce(f32[128]{0:T(128)S(1)} %dynamic-update-slice.12, f32[128]{0:T(128)S(1)} %dynamic-update-slice.8), channel_id=14, replica_groups=mesh['rows_0'=4,'rows_1'=8,'cols_0'=4,'cols_1'=2] {'rows_0'}, use_global_device_ids=true, to_apply=%add.12 | all-reduce | flops 256 | bytes 2048
  170.3 13.8 %all-reduce.25 = (f32[256]{0:T(256)S(1)}, f32[256]{0:T(256)S(1)}) all-reduce(f32[256]{0:T(256)S(1)} %dynamic-update-slice.13, f32[256]{0:T(256)S(1)} %dynamic-update-slice.9), channel_id=15, replica_groups=mesh['rows_0'=4,'rows_1'=8,'cols_0'=4,'cols_1'=2] {'rows_1'}, use_global_device_ids=true, to_apply=%add.13 | all-reduce | flops 512 | bytes 4096
  184.7 7.0 %all-reduce.28 = (f32[128]{0:T(128)S(1)}, f32[128]{0:T(128)S(1)}) all-reduce(f32[128]{0:T(128)S(1)} %dynamic-update-slice.14, f32[128]{0:T(128)S(1)} %dynamic-update-slice.10), channel_id=16, replica_groups=mesh['rows_0'=4,'rows_1'=8,'cols_0'=4,'cols_1'=2] {'cols_0'}, use_global_device_ids=true, to_apply=%add.14 | all-reduce | flops 256 | bytes 2048
  192.5 9.0 %all-reduce.34 = (f32[64]{0:T(128)S(1)}, f32[64]{0:T(128)S(1)}) all-reduce(f32[64]{0:T(128)S(1)} %dynamic-update-slice.15, f32[64]{0:T(128)S(1)} %dynamic-update-slice.11), channel_id=17, replica_groups=mesh['rows_0'=4,'rows_1'=8,'cols_0'=4,'cols_1'=2] {'cols_1'}, use_global_device_ids=true, to_apply=%add.15 | all-reduce | flops 128 | bytes 1024
  202.0 2.1 multiply_convert_fusion.1
  204.5 0.9 slice_select_fusion.1
  206.1 0.9 copy-done.11
  207.0 1.2 fusion.68
  209.1 7.7 %all-reduce.30 = (f32[128]{0:T(128)S(1)}, f32[128]{0:T(128)S(1)}) all-reduce(f32[128]{0:T(128)S(1)} %dynamic-update-slice.20, f32[128]{0:T(128)S(1)} %dynamic-update-slice.16), channel_id=22, replica_groups=mesh['rows_0'=4,'rows_1'=8,'cols_0'=4,'cols_1'=2] {'rows_0'}, use_global_device_ids=true, to_apply=%add.20 | all-reduce | flops 256 | bytes 2048
  217.5 10.7 %all-reduce.24 = (f32[256]{0:T(256)S(1)}, f32[256]{0:T(256)S(1)}) all-reduce(f32[256]{0:T(256)S(1)} %dynamic-update-slice.21, f32[256]{0:T(256)S(1)} %dynamic-update-slice.17), channel_id=23, replica_groups=mesh['rows_0'=4,'rows_1'=8,'cols_0'=4,'cols_1'=2] {'rows_1'}, use_global_device_ids=true, to_apply=%add.21 | all-reduce | flops 512 | bytes 4096
  228.8 6.1 %all-reduce.27 = (f32[128]{0:T(128)S(1)}, f32[128]{0:T(128)S(1)}) all-reduce(f32[128]{0:T(128)S(1)} %dynamic-update-slice.22, f32[128]{0:T(128)S(1)} %dynamic-update-slice.18), channel_id=24, replica_groups=mesh['rows_0'=4,'rows_1'=8,'cols_0'=4,'cols_1'=2] {'cols_0'}, use_global_device_ids=true, to_apply=%add.22 | all-reduce | flops 256 | bytes 2048
  235.6 10.0 %all-reduce.33 = (f32[64]{0:T(128)S(1)}, f32[64]{0:T(128)S(1)}) all-reduce(f32[64]{0:T(128)S(1)} %dynamic-update-slice.23, f32[64]{0:T(128)S(1)} %dynamic-update-slice.19), channel_id=25, replica_groups=mesh['rows_0'=4,'rows_1'=8,'cols_0'=4,'cols_1'=2] {'cols_1'}, use_global_device_ids=true, to_apply=%add.23 | all-reduce | flops 128 | bytes 1024
  247.1 3.6 %collective-permute-start.8 = (bf16[4,1,40,512]{3,2,1,0:T(8,128)(2,1)S(1)}, bf16[4,1,40,512]{3,2,1,0:T(8,128)(2,1)S(1)}, u32[]{:S(2)}, u32[]{:S(2)}) collective-permute-start(bf16[4,1,40,512]{3,2,1,0:T(8,128)(2,1)S(1)} %get-tuple-element.45), channel_id=1, source_target_pairs={{0,8},{8,16},{16,24},{24,32},{32,40},{40,48},{48,56},{56,64},{64,7... | collective-permute-start | bytes 491528 | tf_op jit(solution)/shard_map/ppermute | solution.py:25
  250.7 1.3 collective-permute-start.9
  252.0 1.9 collective-permute-done.8
  254.0 3.8 %collective-permute-done.9 = bf16[4,1,40,512]{3,2,1,0:T(8,128)(2,1)S(1)} collective-permute-done((bf16[4,1,40,512]{3,2,1,0:T(8,128)(2,1)S(1)}, bf16[4,1,40,512]{3,2,1,0:T(8,128)(2,1)S(1)}, u32[]{:S(2)}, u32[]{:S(2)}) %collective-permute-start.9) | collective-permute-done | bytes 163872 | tf_op jit(solution)/shard_map/ppermute | solution.py:26
  257.8 4.6 %collective-permute-start.10 = (bf16[4,4,1,512]{3,2,1,0:T(2,128)(2,1)S(1)}, bf16[4,4,1,512]{3,2,1,0:T(2,128)(2,1)S(1)}, u32[]{:S(2)}, u32[]{:S(2)}) collective-permute-start(bf16[4,4,1,512]{3,2,1,0:T(2,128)(2,1)S(1)} %get-tuple-element.41), channel_id=1, source_target_pairs={{0,1},{1,2},{2,3},{3,4},{4,5},{5,6},{6,7},{8,9},{9,10},{10,11},{11... | collective-permute-start | bytes 49160 | tf_op jit(solution)/shard_map/ppermute | solution.py:25
  262.4 2.1 collective-permute-start.11
  264.6 3.1 %collective-permute-done.11 = bf16[4,4,1,512]{3,2,1,0:T(2,128)(2,1)S(1)} collective-permute-done((bf16[4,4,1,512]{3,2,1,0:T(2,128)(2,1)S(1)}, bf16[4,4,1,512]{3,2,1,0:T(2,128)(2,1)S(1)}, u32[]{:S(2)}, u32[]{:S(2)}) %collective-permute-start.11) | collective-permute-done | bytes 16416 | tf_op jit(solution)/shard_map/ppermute | solution.py:26
  268.1 0.8 copy.70
  270.1 2.9 %fusion.63 = bf16[4,2,8,6,32]{4,2,3,1,0:T(8,128)(2,1)S(1)} fusion(bf16[3,3,3,512,32]{3,4,2,1,0:T(8,128)(2,1)S(1)} %copy-done.13, bf16[6,4,1,7,2,512]{5,3,4,1,0,2:T(8,128)(2,1)S(1)} %slice.111, bf16[6,4,1,8,6,512]{5,3,4,1,0,2:T(8,128)(2,1)S(1)} %copy.66, pred[8,6]{0,1:T(8,128)(4,1)S(1)} %copy-done.22), kind=kOutput, calls=%fused_computation.68 | convolution fusion | flops 344481792 | bytes 2433072 | tf_op jit(solution)/shard_map/conv_general_dilated | solution.py:38
  273.8 1.6 copy.68
  (208 shorter events, 28.0 us)
Async XLA Ops:
  0.0 151.6 %copy-start = (bf16[3,3,3,256,256]{4,3,2,1,0:T(8,128)(2,1)S(1)}, bf16[3,3,3,256,256]{4,3,2,1,0:T(8,128)(2,1)}, u32[]{:S(2)}) copy-start(bf16[3,3,3,256,256]{4,3,2,1,0:T(8,128)(2,1)} %param.15) | copy-start | bytes 10616836
  2.1 26.1 %copy-start.18 = (u32[256]{0:T(256)S(1)}, u32[256]{0:T(256)}, u32[]{:S(2)}) copy-start(u32[256]{0:T(256)} %constant.89) | copy-start | bytes 3076
  2.1 26.8 %copy-start.17 = (u32[256]{0:T(256)S(1)}, u32[256]{0:T(256)}, u32[]{:S(2)}) copy-start(u32[256]{0:T(256)} %constant.94) | copy-start | bytes 3076
  2.1 28.8 %copy-start.16 = (u32[256]{0:T(256)S(1)}, u32[256]{0:T(256)}, u32[]{:S(2)}) copy-start(u32[256]{0:T(256)} %constant.99) | copy-start | bytes 3076
  2.1 29.9 %copy-start.15 = (u32[256]{0:T(256)S(1)}, u32[256]{0:T(256)}, u32[]{:S(2)}) copy-start(u32[256]{0:T(256)} %constant.104) | copy-start | bytes 3076
  2.1 11.2 %collective-permute-start = (bf16[4,2,160,128]{3,2,1,0:T(8,128)(2,1)}, bf16[4,2,160,128]{3,2,1,0:T(8,128)(2,1)}, u32[]{:S(2)}, u32[]{:S(2)}) collective-permute-start(bf16[4,2,160,128]{3,2,1,0:T(8,128)(2,1)} %get-tuple-element.40), channel_id=1, source_target_pairs={{0,8},{8,16},{16,24},{24,32},{32,40},{40,48},{48,56},{56,64},{64,7... | collective-permute-start | bytes 983048 | tf_op jit(solution)/shard_map/ppermute | solution.py:25
  7.4 10.5 %collective-permute-start.1 = (bf16[4,2,160,128]{3,2,1,0:T(8,128)(2,1)}, bf16[4,2,160,128]{3,2,1,0:T(8,128)(2,1)}, u32[]{:S(2)}, u32[]{:S(2)}) collective-permute-start(bf16[4,2,160,128]{3,2,1,0:T(8,128)(2,1)} %get-tuple-element.39), channel_id=1, source_target_pairs={{8,0},{16,8},{24,16},{32,24},{40,32},{48,40},{56,48},{64,56},{72,6... | collective-permute-start | bytes 983048 | tf_op jit(solution)/shard_map/ppermute | solution.py:26
  18.8 1.3 copy-start.3
  20.8 12.4 %collective-permute-start.2 = (bf16[4,12,2,128]{3,2,1,0:T(2,128)(2,1)}, bf16[4,12,2,128]{3,2,1,0:T(2,128)(2,1)}, u32[]{:S(2)}, u32[]{:S(2)}) collective-permute-start(bf16[4,12,2,128]{3,2,1,0:T(2,128)(2,1)} %get-tuple-element.35), channel_id=1, source_target_pairs={{0,1},{1,2},{2,3},{3,4},{4,5},{5,6},{6,7},{8,9},{9,10},{10,11},{11... | collective-permute-start | bytes 73736 | tf_op jit(solution)/shard_map/ppermute | solution.py:25
  25.7 7.6 %collective-permute-start.3 = (bf16[4,12,2,128]{3,2,1,0:T(2,128)(2,1)}, bf16[4,12,2,128]{3,2,1,0:T(2,128)(2,1)}, u32[]{:S(2)}, u32[]{:S(2)}) collective-permute-start(bf16[4,12,2,128]{3,2,1,0:T(2,128)(2,1)} %get-tuple-element.36), channel_id=1, source_target_pairs={{1,0},{2,1},{3,2},{4,3},{5,4},{6,5},{7,6},{9,8},{10,9},{11,10},{12... | collective-permute-start | bytes 73736 | tf_op jit(solution)/shard_map/ppermute | solution.py:26
  28.3 6.1 %copy-start.4 = (bf16[4,12,160,128]{3,2,1,0:T(8,128)(2,1)S(1)}, bf16[4,12,160,128]{3,2,1,0:T(8,128)(2,1)}, u32[]{:S(2)}) copy-start(bf16[4,12,160,128]{3,2,1,0:T(8,128)(2,1)} %copy-done.3) | copy-start | bytes 5898244
  45.1 2.6 copy-start.12
  45.1 2.6 copy-start.19
  59.3 1.6 copy-start.2
  121.2 0.7 copy-start.6
  124.8 1.1 copy-start.14
  124.8 1.1 copy-start.21
  128.0 8.8 %collective-permute-start.4 = (bf16[4,2,80,256]{3,1,2,0:T(2,128)(2,1)S(1)}, bf16[4,2,80,256]{3,1,2,0:T(2,128)(2,1)S(1)}, u32[]{:S(2)}, u32[]{:S(2)}) collective-permute-start(bf16[4,2,80,256]{3,1,2,0:T(2,128)(2,1)S(1)} %get-tuple-element.43), channel_id=1, source_target_pairs={{0,8},{8,16},{16,24},{24,32},{32,40},{40,48},{48,56},{56,64},{64,7... | collective-permute-start | bytes 983048 | tf_op jit(solution)/shard_map/ppermute | solution.py:25
  130.0 10.5 %collective-permute-start.5 = (bf16[4,2,80,256]{3,1,2,0:T(2,128)(2,1)S(1)}, bf16[4,2,80,256]{3,1,2,0:T(2,128)(2,1)S(1)}, u32[]{:S(2)}, u32[]{:S(2)}) collective-permute-start(bf16[4,2,80,256]{3,1,2,0:T(2,128)(2,1)S(1)} %get-tuple-element.44), channel_id=1, source_target_pairs={{8,0},{16,8},{24,16},{32,24},{40,32},{48,40},{56,48},{64,56},{72,6... | collective-permute-start | bytes 983048 | tf_op jit(solution)/shard_map/ppermute | solution.py:26
  140.6 4.8 %collective-permute-start.6 = (bf16[4,8,2,256]{3,1,2,0:T(8,128)(2,1)S(1)}, bf16[4,8,2,256]{3,1,2,0:T(8,128)(2,1)S(1)}, u32[]{:S(2)}, u32[]{:S(2)}) collective-permute-start(bf16[4,8,2,256]{3,1,2,0:T(8,128)(2,1)S(1)} %get-tuple-element.37), channel_id=1, source_target_pairs={{0,1},{1,2},{2,3},{3,4},{4,5},{5,6},{6,7},{8,9},{9,10},{10,11},{11... | collective-permute-start | bytes 98312 | tf_op jit(solution)/shard_map/ppermute | solution.py:25
  143.2 5.2 %collective-permute-start.7 = (bf16[4,8,2,256]{3,1,2,0:T(8,128)(2,1)S(1)}, bf16[4,8,2,256]{3,1,2,0:T(8,128)(2,1)S(1)}, u32[]{:S(2)}, u32[]{:S(2)}) collective-permute-start(bf16[4,8,2,256]{3,1,2,0:T(8,128)(2,1)S(1)} %get-tuple-element.38), channel_id=1, source_target_pairs={{1,0},{2,1},{3,2},{4,3},{5,4},{6,5},{7,6},{9,8},{10,9},{11,10},{12... | collective-permute-start | bytes 98312 | tf_op jit(solution)/shard_map/ppermute | solution.py:26
  151.1 0.7 copy-start.20
  159.0 1.2 copy-start.5
  159.8 42.3 %copy-start.9 = (f32[256]{0:T(256)S(1)}, f32[256]{0:T(256)}, u32[]{:S(2)}) copy-start(f32[256]{0:T(256)} %param.21) | copy-start | bytes 3076
  159.8 42.3 %copy-start.10 = (f32[256]{0:T(256)S(1)}, f32[256]{0:T(256)}, u32[]{:S(2)}) copy-start(f32[256]{0:T(256)} %param.20) | copy-start | bytes 3076
  205.4 1.7 copy-start.11
  205.4 1.7 copy-start.22
  207.0 39.8 %copy-start.7 = (f32[512]{0:T(512)S(1)}, f32[512]{0:T(512)}, u32[]{:S(2)}) copy-start(f32[512]{0:T(512)} %param.23) | copy-start | bytes 6148
  207.0 39.8 %copy-start.8 = (f32[512]{0:T(512)S(1)}, f32[512]{0:T(512)}, u32[]{:S(2)}) copy-start(f32[512]{0:T(512)} %param.22) | copy-start | bytes 6148
  247.1 6.9 %collective-permute-start.8 = (bf16[4,1,40,512]{3,2,1,0:T(8,128)(2,1)S(1)}, bf16[4,1,40,512]{3,2,1,0:T(8,128)(2,1)S(1)}, u32[]{:S(2)}, u32[]{:S(2)}) collective-permute-start(bf16[4,1,40,512]{3,2,1,0:T(8,128)(2,1)S(1)} %get-tuple-element.45), channel_id=1, source_target_pairs={{0,8},{8,16},{16,24},{24,32},{32,40},{40,48},{48,56},{56,64},{64,7... | collective-permute-start | bytes 491528 | tf_op jit(solution)/shard_map/ppermute | solution.py:25
  250.7 7.0 %collective-permute-start.9 = (bf16[4,1,40,512]{3,2,1,0:T(8,128)(2,1)S(1)}, bf16[4,1,40,512]{3,2,1,0:T(8,128)(2,1)S(1)}, u32[]{:S(2)}, u32[]{:S(2)}) collective-permute-start(bf16[4,1,40,512]{3,2,1,0:T(8,128)(2,1)S(1)} %get-tuple-element.46), channel_id=1, source_target_pairs={{8,0},{16,8},{24,16},{32,24},{40,32},{48,40},{56,48},{64,56},{72,6... | collective-permute-start | bytes 491528 | tf_op jit(solution)/shard_map/ppermute | solution.py:26
  257.8 6.8 %collective-permute-start.10 = (bf16[4,4,1,512]{3,2,1,0:T(2,128)(2,1)S(1)}, bf16[4,4,1,512]{3,2,1,0:T(2,128)(2,1)S(1)}, u32[]{:S(2)}, u32[]{:S(2)}) collective-permute-start(bf16[4,4,1,512]{3,2,1,0:T(2,128)(2,1)S(1)} %get-tuple-element.41), channel_id=1, source_target_pairs={{0,1},{1,2},{2,3},{3,4},{4,5},{5,6},{6,7},{8,9},{9,10},{10,11},{11... | collective-permute-start | bytes 49160 | tf_op jit(solution)/shard_map/ppermute | solution.py:25
  262.4 5.2 %collective-permute-start.11 = (bf16[4,4,1,512]{3,2,1,0:T(2,128)(2,1)S(1)}, bf16[4,4,1,512]{3,2,1,0:T(2,128)(2,1)S(1)}, u32[]{:S(2)}, u32[]{:S(2)}) collective-permute-start(bf16[4,4,1,512]{3,2,1,0:T(2,128)(2,1)S(1)} %get-tuple-element.42), channel_id=1, source_target_pairs={{1,0},{2,1},{3,2},{4,3},{5,4},{6,5},{7,6},{9,8},{10,9},{11,10},{12... | collective-permute-start | bytes 49160 | tf_op jit(solution)/shard_map/ppermute | solution.py:26
  268.9 1.2 copy-start.13
  270.1 5.3 %copy-start.1 = (bf16[3,3,3,256,256]{4,3,2,1,0:T(8,128)(2,1)S(1)}, bf16[3,3,3,256,256]{4,3,2,1,0:T(8,128)(2,1)}, u32[]{:S(2)}) copy-start(bf16[3,3,3,256,256]{4,3,2,1,0:T(8,128)(2,1)} %param.15) | copy-start | bytes 10616836
